TPU v7x, 512 devices: a whole 4x8x8 slice. The times are simulated.
512 devices in a mesh: ctx: 16 (over z_lo, y), exp: 32 (over x, z_hi, core).
Axes of the slice: x: 4, y: 8, z: 8 (z_hi: 4, z_lo: 2; z = z_hi * 2 + z_lo), core: 2. Of those that a mesh axis runs over, the one named last changes fastest.
Arguments:
- queries: bfloat16 [2048, 8192], P('ctx', 'exp'), may hold values from -6 to 6
- keys: bfloat16 [2048, 512], P('ctx'), may hold values from -6 to 6
- values: bfloat16 [2048, 512], P('ctx'), may hold values from -5 to 5
- residual: bfloat16 [2048, 4096], P(('ctx', 'exp')), may hold values from -6 to 6
- out_weight: bfloat16 [8192, 4096], P('exp'), may hold values from -0.125 to 0.125
- norm_gain: float32 [4096], replicated, may hold values from 0.25 to 1.75
- expert_ids: int32 [2048, 8], P(('ctx', 'exp')), may hold values from 0 to 31, all different within a row; in each aligned block of 4 rows (0 to 3, 4 to 7, ...) at most 2 rows name the same one
- expert_gates: float32 [2048, 8], P(('ctx', 'exp')), may hold values from 0.05 to 0.35
- w_gate: bfloat16 [32, 4096, 1536], P('exp', None, 'ctx'), may hold values from -0.09375 to 0.09375
- w_up: bfloat16 [32, 4096, 1536], P('exp', None, 'ctx'), may hold values from -0.09375 to 0.09375
- w_down: bfloat16 [32, 1536, 4096], P('exp', None, 'ctx'), may hold values from -0.3125 to 0.3125
Outputs:
- mixed: bfloat16 [2048, 4096], P(('ctx', 'exp'))
- experts_out: bfloat16 [2048, 4096], P(('ctx', 'exp'))
Inputs may be any that keep to these rules, and one draw needn't show every extreme that they name: `expert_ids`: in each aligned block of 4 rows (the rows of one device) no expert is named by more than 2 rows, a bound that some block reaches.
All inputs are finite; a program needn't handle non-finite values.
Results may differ from a plain program's by a relative error of at most 0.034.
Values may be sent and summed in bfloat16 or wider, within the bound.
No kernel may reach another device: no remote copies, remote signals or barrier semaphores. Data moves between devices by JAX's collectives and lax.ppermute only.
A program may use at most 64 MiB of HBM per device.

v0:
```python
import jax
import jax.numpy as jnp
import numpy as np
from jax import lax
from jax.sharding import Mesh, PartitionSpec as P

HEAD_WIDTH = 128
EXTRA = 128
CTX = ("zl", "y")
EXP = ("x", "zh", "co")
EPS_NORM = 1e-06
NEG_LARGE = -1e30


def exchange(pieces, axis):
    return lax.all_to_all(pieces, axis, 0, 0, tiled=True)


def spread(value, axis, count):
    return exchange(jnp.broadcast_to(value[None], (count,) + value.shape), axis)


def added(pieces):
    return jnp.sum(pieces.astype(jnp.float32), axis=0)


def rows_dot(left, right):
    return lax.dot_general(
        left, right, (((1,), (1,)), ((), ())), preferred_element_type=jnp.float32
    )


def route(expert_ids, expert_gates, expert_count, slots):
    flat_ids = expert_ids.reshape(-1)
    tok_rows, top_count = expert_ids.shape
    owner_row = jnp.arange(tok_rows * top_count, dtype=jnp.int32) // top_count
    earlier = (flat_ids[:, None] == flat_ids[None, :]) & (owner_row[None, :] < owner_row[:, None])
    slot_ids = jnp.sum(earlier.astype(jnp.int32), axis=1).reshape(tok_rows, top_count)
    expert_hit = (
        expert_ids[None, None] == jnp.arange(expert_count, dtype=jnp.int32)[:, None, None, None]
    )
    slot_hit = slot_ids[None, None] == jnp.arange(slots, dtype=jnp.int32)[None, :, None, None]
    hits = expert_hit & slot_hit
    table = jnp.any(hits, axis=3).astype(jnp.bfloat16)
    mix = jnp.sum(jnp.where(hits, expert_gates[None, None], 0.0), axis=3)
    return (
        table.reshape(expert_count * slots, tok_rows),
        mix.reshape(expert_count * slots, tok_rows),
    )


def on_device(
    queries,
    keys,
    values,
    residual,
    out_weight,
    norm_gain,
    expert_ids,
    expert_gates,
    w_gate,
    w_up,
    w_down,
):
    n_zl, n_y = (lax.axis_size("zl"), lax.axis_size("y"))
    n_x, n_zh, n_co = (lax.axis_size("x"), lax.axis_size("zh"), lax.axis_size("co"))
    zl, y_pos, x_pos, co = (lax.axis_index(a) for a in ("zl", "y", "x", "co"))
    ctx_count, expert_count = (n_zl * n_y, n_x * n_zh * n_co)
    width = residual.shape[1]
    tok_dev, top_count = expert_ids.shape
    slots = 2
    tok_block = queries.shape[0]
    heads = queries.shape[1] // HEAD_WIDTH
    swap = [(i, n_zl - 1 - i) for i in range(n_zl)]
    gate_up = jnp.stack([w_gate[0].T, w_up[0].T])
    gate_up_other = lax.ppermute(gate_up, "zl", swap)
    down_other = lax.ppermute(w_down[0], "zl", swap)
    mine = jnp.where(co == 0, keys, values)
    mine = lax.dynamic_slice_in_dim(mine, x_pos * HEAD_WIDTH, HEAD_WIDTH, 1)
    gathered = spread(mine, CTX, ctx_count).reshape(ctx_count * tok_block, HEAD_WIDTH)
    key_all, value_all = spread(gathered, "co", n_co)
    order = np.arange(tok_block).reshape(n_x, n_zh, n_co, tok_dev).transpose(2, 0, 1, 3)
    split = queries.reshape(n_x, n_zh, n_co, tok_dev, heads, HEAD_WIDTH)
    query_rows = jnp.transpose(split, (4, 2, 0, 1, 3, 5)).reshape(heads * tok_block, HEAD_WIDTH)
    query_pos = (zl * n_y + y_pos) * tok_block + jnp.asarray(
        np.tile(order.reshape(-1), heads), jnp.int32
    )
    key_pos = jnp.arange(key_all.shape[0], dtype=jnp.int32)
    allowed = key_pos[None, :] <= query_pos[:, None]
    scores = rows_dot(query_rows, key_all) * (1.0 / HEAD_WIDTH**0.5)
    scores = jnp.where(allowed, scores, NEG_LARGE)
    weights = jnp.exp(scores - jnp.max(scores, axis=1, keepdims=True))
    total = jnp.sum(weights, axis=1, keepdims=True)
    numer = jnp.dot(weights.astype(jnp.bfloat16), value_all, preferred_element_type=jnp.float32)
    done = (numer / total).astype(jnp.bfloat16).reshape(heads, tok_block, HEAD_WIDTH)
    heads_out = jnp.transpose(done, (1, 0, 2)).reshape(tok_block, heads * HEAD_WIDTH)
    partial = jnp.dot(heads_out, out_weight, preferred_element_type=jnp.float32)
    partial = partial.astype(jnp.bfloat16).reshape(n_co, tok_block // n_co, width)
    partial = added(exchange(partial, "co")).astype(jnp.bfloat16)
    projected = added(exchange(partial.reshape(n_x * n_zh, tok_dev, width), ("x", "zh")))
    mixed = (residual.astype(jnp.float32) + projected).astype(jnp.bfloat16)
    stream = mixed.astype(jnp.float32)
    mean_sq = jnp.mean(stream * stream, axis=1, keepdims=True)
    normed = (stream * lax.rsqrt(mean_sq + EPS_NORM) * norm_gain[None, :]).astype(jnp.bfloat16)
    table, mix = route(expert_ids, expert_gates, expert_count, slots)
    mix_high = mix.astype(jnp.bfloat16)
    mix_low = (mix - mix_high.astype(jnp.float32)).astype(jnp.bfloat16)
    extra = jnp.concatenate([mix_high, mix_low], axis=1)
    extra = jnp.pad(extra, ((0, 0), (0, EXTRA - extra.shape[1])))
    outgoing = jnp.dot(table, normed, preferred_element_type=jnp.float32).astype(jnp.bfloat16)
    outgoing = jnp.concatenate([outgoing, extra], axis=1)
    arrived = exchange(outgoing.reshape(expert_count, slots, width + EXTRA), EXP)
    rows = lax.all_gather(
        arrived.reshape(expert_count * slots, width + EXTRA), "y", axis=0, tiled=True
    )
    weight_in = jnp.stack([gate_up, gate_up_other], axis=1)
    weight_in = jnp.pad(weight_in, ((0, 0),) * 3 + ((0, EXTRA),)).reshape(-1, width + EXTRA)
    both = rows_dot(weight_in, rows)
    units = both.shape[0] // 2
    hidden = (jax.nn.silu(both[:units]) * both[units:]).astype(jnp.bfloat16)
    hidden = spread(hidden, "y", n_y).reshape(n_y * units, -1)
    down = jnp.concatenate([w_down[0], down_other], axis=1)
    down = down.reshape(n_zl, n_y, units // n_zl, down.shape[1])
    down = jnp.where(zl == 0, down, down[::-1])
    down = jnp.transpose(down, (1, 0, 2, 3)).reshape(n_y * units, -1)
    result = lax.dot_general(
        hidden, down, (((0,), (0,)), ((), ())), preferred_element_type=jnp.float32
    )
    gates = rows[:, width : width + 2 * tok_dev].astype(jnp.float32)
    gates = gates[:, :tok_dev] + gates[:, tok_dev:]
    result = (result * jnp.sum(gates, axis=1, keepdims=True)).astype(jnp.bfloat16)
    block_of = np.arange(n_y * expert_count).reshape(n_y, n_x, n_zh, n_co)
    block_of = block_of.transpose(3, 1, 2, 0).reshape(-1)
    token_of = (block_of[:, None] * tok_dev + np.arange(tok_dev)[None, :]).reshape(-1)
    place = jnp.sum(
        (gates != 0).astype(jnp.int32) * jnp.arange(1, tok_dev + 1, dtype=jnp.int32)[None, :],
        axis=1,
    )
    slot_block = jnp.arange(n_y * expert_count * slots, dtype=jnp.int32) // slots
    slot_token = jnp.where(place > 0, slot_block * tok_dev + place - 1, -1)
    onehot = (jnp.asarray(token_of, jnp.int32)[:, None] == slot_token[None, :]).astype(jnp.bfloat16)
    tokens = jnp.dot(onehot, result, preferred_element_type=jnp.float32).astype(jnp.bfloat16)
    cols = tokens.shape[1]
    tokens = added(exchange(tokens.reshape(n_co, -1, cols), "co")).astype(jnp.bfloat16)
    tokens = added(exchange(tokens.reshape(n_x, -1, cols), "x")).astype(jnp.bfloat16)
    tokens = exchange(tokens.reshape(n_zh * n_y, tok_dev, cols), ("zh", "y"))
    tokens = added(tokens.reshape(n_zh, n_y, tok_dev, cols))
    tokens = tokens.reshape(n_y, tok_dev, n_zl, cols // n_zl).transpose(1, 2, 0, 3)
    tokens = jnp.where(zl == 0, tokens, tokens[:, ::-1])
    return (mixed, tokens.reshape(tok_dev, width).astype(jnp.bfloat16))


def solution(mesh):
    fine = Mesh(mesh.devices.reshape(2, 8, 4, 4, 2), CTX + EXP)
    return jax.shard_map(
        on_device,
        mesh=fine,
        in_specs=(
            P(CTX, EXP),
            P(CTX, None),
            P(CTX, None),
            P(CTX + EXP, None),
            P(EXP, None),
            P(),
            P(CTX + EXP, None),
            P(CTX + EXP, None),
            P(EXP, None, CTX),
            P(EXP, None, CTX),
            P(EXP, None, CTX),
        ),
        out_specs=(P(CTX + EXP, None), P(CTX + EXP, None)),
        check_vma=False,
    )
```

profile of v0, /device:TPU:8, one launch (start us, length us, event | category | flops | bytes accessed | tf_op | source)
XLA Modules:
  0.0 259.2 jit_solution(8927563244535573260)
XLA Ops:
  7.2 0.9 dynamic-slice_select_fusion
  8.1 0.9 broadcast_in_dim.21
  9.0 9.4 %all-to-all-start = ((bf16[16,128,128]{2,1,0:T(8,128)(2,1)}), bf16[16,128,128]{2,1,0:T(8,128)(2,1)S(1)}, u32[]{:S(2)}, u32[]{:S(2)}) async-start(bf16[16,128,128]{2,1,0:T(8,128)(2,1)} %broadcast_in_dim.21), calls=%async_computation | async-start | bytes 1048576 | tf_op jit(solution)/shard_map/all_to_all | solution.py:16
  18.4 0.9 reshape.150
  19.3 0.8 eq.79
  20.0 0.2 convert_reduce_fusion.2
  20.3 0.7 broadcast_add_fusion
  21.0 12.4 %all-to-all-done = bf16[16,128,128]{2,1,0:T(8,128)(2,1)S(1)} async-done(((bf16[16,128,128]{2,1,0:T(8,128)(2,1)}), bf16[16,128,128]{2,1,0:T(8,128)(2,1)S(1)}, u32[]{:S(2)}, u32[]{:S(2)}) %all-to-all-start) | async-done | bytes 524320 | tf_op jit(solution)/shard_map/all_to_all | solution.py:16
  33.4 4.6 %all_to_all.45 = bf16[2,2048,128]{2,1,0:T(8,128)(2,1)S(1)} all-to-all(bf16[2,2048,128]{2,1,0:T(8,128)(2,1)S(1)} %broadcast_in_dim.23), channel_id=1, replica_groups=mesh['zl'=2,'y'=8,'x'=4,'zh'=4,'co'=2] {'co'}, dimensions={0} | all-to-all | bytes 2097152 | tf_op jit(solution)/shard_map/all_to_all | solution.py:16
  38.0 0.5 fusion.39
  38.5 0.4 fusion.7
  38.9 0.5 fusion.14
  39.6 0.5 convolution_convert_fusion
  40.0 4.6 %all_to_all.46 = bf16[2,64,4096]{2,1,0:T(8,128)(2,1)S(1)} all-to-all(bf16[2,64,4096]{2,1,0:T(8,128)(2,1)S(1)} %bitcast.69), channel_id=1, replica_groups=mesh['zl'=2,'y'=8,'x'=4,'zh'=4,'co'=2] {'co'}, dimensions={0} | all-to-all | bytes 2097152 | tf_op jit(solution)/shard_map/all_to_all | solution.py:16
  44.6 1.1 reduce_sum.109
  45.7 2.0 reshape.155
  47.8 12.0 %all-to-all-start.3 = ((bf16[16,4,4096]{2,1,0:T(4,128)(2,1)}), bf16[16,4,4096]{2,1,0:T(4,128)(2,1)S(1)}, u32[]{:S(2)}, u32[]{:S(2)}) async-start(bf16[16,4,4096]{2,1,0:T(4,128)(2,1)} %reshape.155), calls=%async_computation.3 | async-start | bytes 1048576 | tf_op jit(solution)/shard_map/all_to_all | solution.py:16
  60.7 15.6 %all-to-all-done.3 = bf16[16,4,4096]{2,1,0:T(4,128)(2,1)S(1)} async-done(((bf16[16,4,4096]{2,1,0:T(4,128)(2,1)}), bf16[16,4,4096]{2,1,0:T(4,128)(2,1)S(1)}, u32[]{:S(2)}, u32[]{:S(2)}) %all-to-all-start.3) | async-done | bytes 524320 | tf_op jit(solution)/shard_map/all_to_all | solution.py:16
  76.3 0.4 convert_reduce_fusion
  76.7 0.2 fusion.24
  76.9 0.3 convolution_convert_fusion.1
  77.3 0.2 reshape.158
  77.5 23.2 %all_to_all.47 = bf16[32,2,4224]{2,1,0:T(2,128)(2,1)S(1)} all-to-all(bf16[32,2,4224]{2,1,0:T(2,128)(2,1)S(1)} %reshape.158), channel_id=1, replica_groups=mesh['zl'=2,'y'=8,'x'=4,'zh'=4,'co'=2] {'x','zh','co'}, dimensions={0} | all-to-all | bytes 1081344 | tf_op jit(solution)/shard_map/all_to_all | solution.py:16
  100.7 1.0 reshape.159
  101.9 1.3 fusion.38
  103.3 5.0 %collective-permute-start = (bf16[2,96,4096]{2,1,0:T(8,128)(2,1)S(1)}, bf16[2,96,4096]{2,1,0:T(8,128)(2,1)S(1)}, u32[]{:S(2)}, u32[]{:S(2)}) collective-permute-start(bf16[2,96,4096]{2,1,0:T(8,128)(2,1)S(1)} %get-tuple-element.7), channel_id=1, source_target_pairs={{0,256},{256,0},{1,257},{257,1},{2,258},{258,2},{3,259},{259,3},{4... | collective-permute-start | bytes 4718600 | tf_op jit(solution)/shard_map/ppermute | solution.py:76
  108.3 34.6 %collective-permute-done = bf16[2,96,4096]{2,1,0:T(8,128)(2,1)S(1)} collective-permute-done((bf16[2,96,4096]{2,1,0:T(8,128)(2,1)S(1)}, bf16[2,96,4096]{2,1,0:T(8,128)(2,1)S(1)}, u32[]{:S(2)}, u32[]{:S(2)}) %collective-permute-start) | collective-permute-done | bytes 1572896 | tf_op jit(solution)/shard_map/ppermute | solution.py:76
  142.9 2.0 fusion.2
  144.9 8.5 %all-gather.2.cloned.1.call-done = bf16[512,4224]{1,0:T(8,128)(2,1)} async-done(((bf16[64,4224]{1,0:T(8,128)(2,1)}), bf16[512,4224]{1,0:T(8,128)(2,1)}) %all-gather.2.cloned.1.call-update) | async-done | bytes 4325392 | tf_op jit(solution)/shard_map/all_gather | solution.py:113
  153.4 5.1 %fusion.40 = f32[384,512]{1,0:T(8,128)S(1)} fusion(bf16[384,4224]{1,0:T(8,128)(2,1)} %bitcast.70, bf16[512,4224]{1,0:T(8,128)(2,1)} %all-gather.2.cloned.1.call-done), kind=kOutput, calls=%fused_computation.80 | convolution fusion | flops 1660944384 | bytes 8355840 | tf_op jit(solution)/shard_map/dot_general | solution.py:28
  158.7 1.3 broadcast_in_dim.31
  160.0 6.4 %all-to-all-start.5 = ((bf16[8,192,512]{2,1,0:T(8,128)(2,1)}), bf16[8,192,512]{2,1,0:T(8,128)(2,1)}, u32[]{:S(2)}, u32[]{:S(2)}) async-start(bf16[8,192,512]{2,1,0:T(8,128)(2,1)} %broadcast_in_dim.31), calls=%async_computation.5 | async-start | bytes 3145728 | tf_op jit(solution)/shard_map/all_to_all | solution.py:16
  166.4 3.5 %collective-permute-start.1 = (bf16[1536,256]{1,0:T(8,128)(2,1)S(1)}, bf16[1536,256]{1,0:T(8,128)(2,1)}, u32[]{:S(2)}, u32[]{:S(2)}) collective-permute-start(bf16[1536,256]{1,0:T(8,128)(2,1)S(1)} %bitcast.78), channel_id=1, source_target_pairs={{0,256},{256,0},{1,257},{257,1},{2,258},{258,2},{3,259},{259,3},{4... | collective-permute-start | bytes 2359304 | tf_op jit(solution)/shard_map/ppermute | solution.py:77
  169.9 17.1 %collective-permute-done.1 = bf16[1536,256]{1,0:T(8,128)(2,1)} collective-permute-done((bf16[1536,256]{1,0:T(8,128)(2,1)S(1)}, bf16[1536,256]{1,0:T(8,128)(2,1)}, u32[]{:S(2)}, u32[]{:S(2)}) %collective-permute-start.1) | collective-permute-done | bytes 786464 | tf_op jit(solution)/shard_map/ppermute | solution.py:77
  187.1 1.3 pad_maximum_fusion.1
  188.3 0.3 fusion.9
  188.7 1.4 copy.86
  190.0 0.9 slice_convert_fusion
  191.0 0.2 fusion.23
  191.2 0.2 select_reduce_fusion
  191.4 13.5 %all-to-all-done.5 = bf16[8,192,512]{2,1,0:T(8,128)(2,1)} async-done(((bf16[8,192,512]{2,1,0:T(8,128)(2,1)}), bf16[8,192,512]{2,1,0:T(8,128)(2,1)}, u32[]{:S(2)}, u32[]{:S(2)}) %all-to-all-start.5) | async-done | bytes 1572896 | tf_op jit(solution)/shard_map/all_to_all | solution.py:16
  205.0 4.5 %fusion.10 = bf16[1024,512]{1,0:T(8,128)(2,1)} fusion(s32[512]{0:T(512)S(1)} %fusion.34, s32[1024]{0:T(1024)S(1)} %copy-done.8, bf16[1536,512]{1,0:T(8,128)(2,1)} %bitcast.21, bf16[1536,512]{1,0:T(8,128)(2,1)} %bitcast.73, f32[512]{0:T(512)S(1)} %fusion.23), kind=kOutput, calls=%fused_computation.19 | convolution fusion | flops 1343750144 | bytes 4202496 | tf_op jit(solution)/shard_map/dot_general | solution.py:142
  209.5 5.7 %all_to_all.48 = bf16[2,512,512]{2,1,0:T(8,128)(2,1)S(1)} all-to-all(bf16[2,512,512]{2,1,0:T(8,128)(2,1)} %bitcast.75), channel_id=1, replica_groups=mesh['zl'=2,'y'=8,'x'=4,'zh'=4,'co'=2] {'co'}, dimensions={0} | all-to-all | bytes 2097152 | tf_op jit(solution)/shard_map/all_to_all | solution.py:16
  215.2 1.1 reduce_sum.116
  216.3 14.0 %all_to_all.49 = bf16[4,128,512]{2,1,0:T(8,128)(2,1)S(1)} all-to-all(bf16[4,128,512]{2,1,0:T(8,128)(2,1)} %bitcast.72), channel_id=1, replica_groups=mesh['zl'=2,'y'=8,'x'=4,'zh'=4,'co'=2] {'x'}, dimensions={0} | all-to-all | bytes 1048576 | tf_op jit(solution)/shard_map/all_to_all | solution.py:16
  230.4 20.9 %all_to_all.50 = bf16[32,4,512]{2,1,0:T(4,128)(2,1)S(1)} all-to-all(bf16[32,4,512]{2,1,0:T(4,128)(2,1)S(1)} %reshape.165), channel_id=1, replica_groups=mesh['zl'=2,'y'=8,'x'=4,'zh'=4,'co'=2] {'zh','y'}, dimensions={0} | all-to-all | bytes 262144 | tf_op jit(solution)/shard_map/all_to_all | solution.py:16
  251.4 0.2 rev.7
  251.7 0.6 copy.92
  (47 shorter events, 1.7 us)
Async XLA Ops:
  7.2 32.4 %copy-start = (bf16[256,4096]{1,0:T(8,128)(2,1)S(1)}, bf16[256,4096]{1,0:T(8,128)(2,1)}, u32[]{:S(2)}) copy-start(bf16[256,4096]{1,0:T(8,128)(2,1)} %param.17) | copy-start | bytes 6291460
  9.0 24.4 %all-to-all-start = ((bf16[16,128,128]{2,1,0:T(8,128)(2,1)}), bf16[16,128,128]{2,1,0:T(8,128)(2,1)S(1)}, u32[]{:S(2)}, u32[]{:S(2)}) async-start(bf16[16,128,128]{2,1,0:T(8,128)(2,1)} %broadcast_in_dim.21), calls=%async_computation | async-start | bytes 1048576 | tf_op jit(solution)/shard_map/all_to_all | solution.py:16
  44.6 15.2 %copy-start.6 = (s32[4,8]{1,0:T(4,128)S(1)}, s32[4,8]{1,0:T(4,128)}, u32[]{:S(2)}) copy-start(s32[4,8]{1,0:T(4,128)} %param.19) | copy-start | bytes 388
  44.6 15.6 %copy-start.7 = (f32[4,8]{1,0:T(4,128)S(1)}, f32[4,8]{1,0:T(4,128)}, u32[]{:S(2)}) copy-start(f32[4,8]{1,0:T(4,128)} %param.20) | copy-start | bytes 388
  44.6 32.1 %copy-start.4 = (bf16[4,4096]{1,0:T(4,128)(2,1)S(1)}, bf16[4,4096]{1,0:T(4,128)(2,1)}, u32[]{:S(2)}) copy-start(bf16[4,4096]{1,0:T(4,128)(2,1)} %param.16) | copy-start | bytes 98308
  44.6 32.3 %copy-start.5 = (f32[4096]{0:T(1024)S(1)}, f32[4096]{0:T(1024)}, u32[]{:S(2)}) copy-start(f32[4096]{0:T(1024)} %param.18) | copy-start | bytes 49156
  47.8 28.5 %all-to-all-start.3 = ((bf16[16,4,4096]{2,1,0:T(4,128)(2,1)}), bf16[16,4,4096]{2,1,0:T(4,128)(2,1)S(1)}, u32[]{:S(2)}, u32[]{:S(2)}) async-start(bf16[16,4,4096]{2,1,0:T(4,128)(2,1)} %reshape.155), calls=%async_computation.3 | async-start | bytes 1048576 | tf_op jit(solution)/shard_map/all_to_all | solution.py:16
  59.8 93.6 %all-gather.2.cloned.1.call-start = ((), (), s32[]{:S(2)}) async-start(), calls=%async_computation.9 | async-start | bytes 4866048 | tf_op jit(solution)/shard_map/all_gather | solution.py:113
  76.9 24.9 %copy-start.3 = (bf16[4,4096]{1,0:T(4,128)(2,1)}, bf16[4,4096]{1,0:T(4,128)(2,1)S(1)}, u32[]{:S(2)}) copy-start(bf16[4,4096]{1,0:T(4,128)(2,1)S(1)} %get-tuple-element.3) | copy-start | bytes 98308
  100.7 1.2 copy-start.1
  103.3 39.7 %collective-permute-start = (bf16[2,96,4096]{2,1,0:T(8,128)(2,1)S(1)}, bf16[2,96,4096]{2,1,0:T(8,128)(2,1)S(1)}, u32[]{:S(2)}, u32[]{:S(2)}) collective-permute-start(bf16[2,96,4096]{2,1,0:T(8,128)(2,1)S(1)} %get-tuple-element.7), channel_id=1, source_target_pairs={{0,256},{256,0},{1,257},{257,1},{2,258},{258,2},{3,259},{259,3},{4... | collective-permute-start | bytes 4718600 | tf_op jit(solution)/shard_map/ppermute | solution.py:76
  158.7 7.7 %copy-start.2 = (bf16[1,1536,256]{2,1,0:T(8,128)(2,1)S(1)}, bf16[1,1536,256]{2,1,0:T(8,128)(2,1)}, u32[]{:S(2)}) copy-start(bf16[1,1536,256]{2,1,0:T(8,128)(2,1)} %param.23) | copy-start | bytes 2359300
  160.0 45.0 %all-to-all-start.5 = ((bf16[8,192,512]{2,1,0:T(8,128)(2,1)}), bf16[8,192,512]{2,1,0:T(8,128)(2,1)}, u32[]{:S(2)}, u32[]{:S(2)}) async-start(bf16[8,192,512]{2,1,0:T(8,128)(2,1)} %broadcast_in_dim.31), calls=%async_computation.5 | async-start | bytes 3145728 | tf_op jit(solution)/shard_map/all_to_all | solution.py:16
  166.4 20.7 %collective-permute-start.1 = (bf16[1536,256]{1,0:T(8,128)(2,1)S(1)}, bf16[1536,256]{1,0:T(8,128)(2,1)}, u32[]{:S(2)}, u32[]{:S(2)}) collective-permute-start(bf16[1536,256]{1,0:T(8,128)(2,1)S(1)} %bitcast.78), channel_id=1, source_target_pairs={{0,256},{256,0},{1,257},{257,1},{2,258},{258,2},{3,259},{259,3},{4... | collective-permute-start | bytes 2359304 | tf_op jit(solution)/shard_map/ppermute | solution.py:77
  188.7 16.3 %copy-start.8 = (s32[1024]{0:T(1024)S(1)}, s32[1024]{0:T(1024)}, u32[]{:S(2)}) copy-start(s32[1024]{0:T(1024)} %constant.94.clone) | copy-start | bytes 12292
Sparse Core Ops, SparseCore 0:
  101.9 51.4 all-gather.1
where the time goes:
time: 260 us; the launch traced here: 259 us
  waiting for transfers between devices  102 us (39%)
  blocking collectives  73 us (28%)
  starting transfers between devices  36.4 us (14%)
  between operations  14.3 us (6%)
  other arithmetic  11.8 us (5%)
  matrix products  11.5 us (4%)
  local copies, waits for them, and re-layouts  10.4 us (4%)
    all_to_all x6, blocking collectives, exchange(): return lax.all_to_all(pieces, axis, 0, 0, tiled=True)  73 us
    all_to_all x3, waiting for transfers between devices, exchange(): return lax.all_to_all(pieces, axis, 0, 0, tiled=True)  41.5 us
    ppermute x1, waiting for transfers between devices, on_device(): gate_up_other = lax.ppermute(gate_up, 'zl', swap)  34.6 us
    all_to_all x3, starting transfers between devices, exchange(): return lax.all_to_all(pieces, axis, 0, 0, tiled=True)  27.7 us
    ppermute x1, waiting for transfers between devices, on_device(): down_other = lax.ppermute(w_down[0], 'zl', swap)  17.1 us
    all_gather x1, waiting for transfers between devices, on_device(): lax.all_gather(arrived.reshape(expert_count * slots, width + EXTRA), 'y',...  8.52 us
    dot_general x2, matrix products, rows_dot(): lax.dot_general(left, right, (((1,), (1,)), ((), ())), preferred_element_...  5.64 us
  transfers between devices with their start and end apart: 6, of which 6 were waited for; matrix products, arithmetic and copies ran while one was open for 4% of the time, Pallas kernels for 0%

commit v1 on v0

--- a/solution.py
+++ b/solution.py
@@ -110,8 +110,14 @@
     outgoing = jnp.dot(table, normed, preferred_element_type=jnp.float32).astype(jnp.bfloat16)
     outgoing = jnp.concatenate([outgoing, extra], axis=1)
     arrived = exchange(outgoing.reshape(expert_count, slots, width + EXTRA), EXP)
-    rows = lax.all_gather(
-        arrived.reshape(expert_count * slots, width + EXTRA), "y", axis=0, tiled=True
+    rows = jnp.concatenate(
+        lax.all_to_all(
+            jnp.stack([arrived.reshape(expert_count * slots, width + EXTRA)] * lax.axis_size("y")),
+            "y",
+            0,
+            0,
+        ),
+        axis=0,
     )
     weight_in = jnp.stack([gate_up, gate_up_other], axis=1)
     weight_in = jnp.pad(weight_in, ((0, 0),) * 3 + ((0, EXTRA),)).reshape(-1, width + EXTRA)

time: 260 us -> 297 us (1.14)
  waiting for transfers between devices: 102 us -> 149 us
  between operations: 14.3 us -> 0.94 us
  local copies, waits for them, and re-layouts: 10.4 us -> 14 us
  starting transfers between devices: 36.4 us -> 39.5 us
    all_to_all x0 -> x1, waiting for transfers between devices: none -> 56.8 us  [on_device(): lax.all_to_all(jnp.stack([arrived.reshape(expert_count * slots, width + E...]
    all_gather x1 -> x0, waiting for transfers between devices: 8.52 us -> none  [on_device(): lax.all_gather(arrived.reshape(expert_count * slots, width + EXTRA), 'y',...]
    all_to_all x0 -> x1, starting transfers between devices: none -> 7.07 us  [on_device(): lax.all_to_all(jnp.stack([arrived.reshape(expert_count * slots, width + E...]
    another operation x0 -> x2, local copies, waits for them, and re-layouts: none -> 3.78 us  [on_device(): jnp.stack([arrived.reshape(expert_count * slots, width + EXTRA)] * lax.ax...]
where the time goes in v1:
time: 297 us; the launch traced here: 296 us
  waiting for transfers between devices  149 us (50%)
  blocking collectives  70.1 us (24%)
  starting transfers between devices  39.5 us (13%)
  local copies, waits for them, and re-layouts  14 us (5%)
  matrix products  11.5 us (4%)
  other arithmetic  10.6 us (4%)
    all_to_all x6, blocking collectives, exchange(): return lax.all_to_all(pieces, axis, 0, 0, tiled=True)  70.1 us
    all_to_all x1, waiting for transfers between devices, on_device(): lax.all_to_all(jnp.stack([arrived.reshape(expert_count * slots, width + E...  56.8 us
    all_to_all x3, waiting for transfers between devices, exchange(): return lax.all_to_all(pieces, axis, 0, 0, tiled=True)  40 us
    ppermute x1, waiting for transfers between devices, on_device(): gate_up_other = lax.ppermute(gate_up, 'zl', swap)  35.1 us
    all_to_all x3, starting transfers between devices, exchange(): return lax.all_to_all(pieces, axis, 0, 0, tiled=True)  27.1 us
    ppermute x1, waiting for transfers between devices, on_device(): down_other = lax.ppermute(w_down[0], 'zl', swap)  17.5 us
    all_to_all x1, starting transfers between devices, on_device(): lax.all_to_all(jnp.stack([arrived.reshape(expert_count * slots, width + E...  7.07 us
  transfers between devices with their start and end apart: 6, of which 6 were waited for; matrix products, arithmetic and copies ran while one was open for 4% of the time, Pallas kernels for 0%

profile of v1, /device:TPU:8, one launch (start us, length us, event | category | flops | bytes accessed | tf_op | source)
XLA Modules:
  0.0 296.0 jit_solution(15440763622815049772)
XLA Ops:
  0.7 0.9 dynamic-slice_select_fusion
  1.6 0.9 broadcast_in_dim.21
  2.5 9.4 %all-to-all-start = ((bf16[16,128,128]{2,1,0:T(8,128)(2,1)}), bf16[16,128,128]{2,1,0:T(8,128)(2,1)S(1)}, u32[]{:S(2)}, u32[]{:S(2)}) async-start(bf16[16,128,128]{2,1,0:T(8,128)(2,1)} %broadcast_in_dim.21), calls=%async_computation | async-start | bytes 1048576 | tf_op jit(solution)/shard_map/all_to_all | solution.py:16
  11.9 0.9 reshape.152
  12.7 0.8 eq.79
  13.5 0.2 convert_reduce_fusion.2
  13.8 0.7 broadcast_add_fusion
  14.5 12.4 %all-to-all-done = bf16[16,128,128]{2,1,0:T(8,128)(2,1)S(1)} async-done(((bf16[16,128,128]{2,1,0:T(8,128)(2,1)}), bf16[16,128,128]{2,1,0:T(8,128)(2,1)S(1)}, u32[]{:S(2)}, u32[]{:S(2)}) %all-to-all-start) | async-done | bytes 524320 | tf_op jit(solution)/shard_map/all_to_all | solution.py:16
  26.9 4.6 %all_to_all.50 = bf16[2,2048,128]{2,1,0:T(8,128)(2,1)S(1)} all-to-all(bf16[2,2048,128]{2,1,0:T(8,128)(2,1)S(1)} %broadcast_in_dim.23), channel_id=1, replica_groups=mesh['zl'=2,'y'=8,'x'=4,'zh'=4,'co'=2] {'co'}, dimensions={0} | all-to-all | bytes 2097152 | tf_op jit(solution)/shard_map/all_to_all | solution.py:16
  31.5 0.5 fusion.39
  32.0 0.4 fusion.7
  32.4 0.5 fusion.14
  33.0 0.5 convolution_convert_fusion
  33.5 4.6 %all_to_all.51 = bf16[2,64,4096]{2,1,0:T(8,128)(2,1)S(1)} all-to-all(bf16[2,64,4096]{2,1,0:T(8,128)(2,1)S(1)} %bitcast.70), channel_id=1, replica_groups=mesh['zl'=2,'y'=8,'x'=4,'zh'=4,'co'=2] {'co'}, dimensions={0} | all-to-all | bytes 2097152 | tf_op jit(solution)/shard_map/all_to_all | solution.py:16
  38.1 1.1 reduce_sum.109
  39.2 2.0 reshape.157
  41.2 12.0 %all-to-all-start.3 = ((bf16[16,4,4096]{2,1,0:T(4,128)(2,1)}), bf16[16,4,4096]{2,1,0:T(4,128)(2,1)S(1)}, u32[]{:S(2)}, u32[]{:S(2)}) async-start(bf16[16,4,4096]{2,1,0:T(4,128)(2,1)} %reshape.157), calls=%async_computation.3 | async-start | bytes 1048576 | tf_op jit(solution)/shard_map/all_to_all | solution.py:16
  54.1 15.7 %all-to-all-done.3 = bf16[16,4,4096]{2,1,0:T(4,128)(2,1)S(1)} async-done(((bf16[16,4,4096]{2,1,0:T(4,128)(2,1)}), bf16[16,4,4096]{2,1,0:T(4,128)(2,1)S(1)}, u32[]{:S(2)}, u32[]{:S(2)}) %all-to-all-start.3) | async-done | bytes 524320 | tf_op jit(solution)/shard_map/all_to_all | solution.py:16
  69.8 0.4 convert_reduce_fusion
  70.2 0.2 fusion.23
  70.4 0.3 convolution_convert_fusion.1
  70.8 0.2 reshape.160
  71.0 23.3 %all_to_all.52 = bf16[32,2,4224]{2,1,0:T(2,128)(2,1)} all-to-all(bf16[32,2,4224]{2,1,0:T(2,128)(2,1)S(1)} %reshape.160), channel_id=1, replica_groups=mesh['zl'=2,'y'=8,'x'=4,'zh'=4,'co'=2] {'x','zh','co'}, dimensions={0} | all-to-all | bytes 1081344 | tf_op jit(solution)/shard_map/all_to_all | solution.py:16
  94.3 1.3 stack_reshape.2
  95.6 2.5 stack.21
  98.1 7.1 %all-to-all-start.5 = ((bf16[8,64,4224]{2,1,0:T(8,128)(2,1)}), bf16[8,64,4224]{2,1,0:T(8,128)(2,1)}, u32[]{:S(2)}, u32[]{:S(2)}) async-start(bf16[8,64,4224]{2,1,0:T(8,128)(2,1)} %stack.21), calls=%async_computation.5 | async-start | bytes 8650752 | tf_op jit(solution)/shard_map/all_to_all | solution.py:114
  105.2 1.3 fusion.38
  106.5 2.6 collective-permute-start
  109.2 35.1 %collective-permute-done = bf16[2,96,4096]{2,1,0:T(8,128)(2,1)S(1)} collective-permute-done((bf16[2,96,4096]{2,1,0:T(8,128)(2,1)S(1)}, bf16[2,96,4096]{2,1,0:T(8,128)(2,1)S(1)}, u32[]{:S(2)}, u32[]{:S(2)}) %collective-permute-start) | collective-permute-done | bytes 1572896 | tf_op jit(solution)/shard_map/ppermute | solution.py:76
  144.2 2.0 fusion.2
  146.2 56.8 %all-to-all-done.5 = bf16[8,64,4224]{2,1,0:T(8,128)(2,1)} async-done(((bf16[8,64,4224]{2,1,0:T(8,128)(2,1)}), bf16[8,64,4224]{2,1,0:T(8,128)(2,1)}, u32[]{:S(2)}, u32[]{:S(2)}) %all-to-all-start.5) | async-done | bytes 4325408 | tf_op jit(solution)/shard_map/all_to_all | solution.py:114
  203.0 5.1 %fusion.40 = f32[384,512]{1,0:T(8,128)S(1)} fusion(bf16[384,4224]{1,0:T(8,128)(2,1)} %bitcast.71, bf16[512,4224]{1,0:T(8,128)(2,1)} %bitcast.11), kind=kOutput, calls=%fused_computation.79 | convolution fusion | flops 1660944384 | bytes 8355840 | tf_op jit(solution)/shard_map/dot_general | solution.py:28
  208.3 1.3 broadcast_in_dim.31
  209.6 5.8 %all-to-all-start.6 = ((bf16[8,192,512]{2,1,0:T(8,128)(2,1)}), bf16[8,192,512]{2,1,0:T(8,128)(2,1)}, u32[]{:S(2)}, u32[]{:S(2)}) async-start(bf16[8,192,512]{2,1,0:T(8,128)(2,1)} %broadcast_in_dim.31), calls=%async_computation.6 | async-start | bytes 3145728 | tf_op jit(solution)/shard_map/all_to_all | solution.py:16
  215.4 2.7 collective-permute-start.1
  218.1 17.5 %collective-permute-done.1 = bf16[1536,256]{1,0:T(8,128)(2,1)} collective-permute-done((bf16[1536,256]{1,0:T(8,128)(2,1)S(1)}, bf16[1536,256]{1,0:T(8,128)(2,1)}, u32[]{:S(2)}, u32[]{:S(2)}) %collective-permute-start.1) | collective-permute-done | bytes 786464 | tf_op jit(solution)/shard_map/ppermute | solution.py:77
  235.6 1.3 pad_maximum_fusion.1
  236.9 0.3 fusion.9
  237.2 1.4 copy.99
  238.6 0.9 slice.20
  239.7 12.0 %all-to-all-done.6 = bf16[8,192,512]{2,1,0:T(8,128)(2,1)} async-done(((bf16[8,192,512]{2,1,0:T(8,128)(2,1)}), bf16[8,192,512]{2,1,0:T(8,128)(2,1)}, u32[]{:S(2)}, u32[]{:S(2)}) %all-to-all-start.6) | async-done | bytes 1572896 | tf_op jit(solution)/shard_map/all_to_all | solution.py:16
  251.7 4.5 %fusion.10 = bf16[1024,512]{1,0:T(8,128)(2,1)} fusion(s32[512]{0:T(512)S(1)} %fusion.33, s32[1024]{0:T(1024)S(1)} %copy-done.8, bf16[1536,512]{1,0:T(8,128)(2,1)} %bitcast.22, bf16[1536,512]{1,0:T(8,128)(2,1)} %bitcast.74, f32[512]{0:T(512)S(1)} %fusion.37), kind=kOutput, calls=%fused_computation.19 | convolution fusion | flops 1343750144 | bytes 4202496 | tf_op jit(solution)/shard_map/dot_general | solution.py:148
  256.2 5.7 %all_to_all.53 = bf16[2,512,512]{2,1,0:T(8,128)(2,1)S(1)} all-to-all(bf16[2,512,512]{2,1,0:T(8,128)(2,1)} %bitcast.76), channel_id=1, replica_groups=mesh['zl'=2,'y'=8,'x'=4,'zh'=4,'co'=2] {'co'}, dimensions={0} | all-to-all | bytes 2097152 | tf_op jit(solution)/shard_map/all_to_all | solution.py:16
  261.9 1.1 reduce_sum.116
  263.0 15.6 %all_to_all.54 = bf16[4,128,512]{2,1,0:T(8,128)(2,1)S(1)} all-to-all(bf16[4,128,512]{2,1,0:T(8,128)(2,1)} %bitcast.73), channel_id=1, replica_groups=mesh['zl'=2,'y'=8,'x'=4,'zh'=4,'co'=2] {'x'}, dimensions={0} | all-to-all | bytes 1048576 | tf_op jit(solution)/shard_map/all_to_all | solution.py:16
  278.8 16.3 %all_to_all.55 = bf16[32,4,512]{2,1,0:T(4,128)(2,1)S(1)} all-to-all(bf16[32,4,512]{2,1,0:T(4,128)(2,1)S(1)} %reshape.167), channel_id=1, replica_groups=mesh['zl'=2,'y'=8,'x'=4,'zh'=4,'co'=2] {'zh','y'}, dimensions={0} | all-to-all | bytes 262144 | tf_op jit(solution)/shard_map/all_to_all | solution.py:16
  295.1 0.2 rev.7
  295.4 0.6 copy.106
  (49 shorter events, 1.7 us)
Async XLA Ops:
  0.6 32.4 %copy-start = (bf16[256,4096]{1,0:T(8,128)(2,1)S(1)}, bf16[256,4096]{1,0:T(8,128)(2,1)}, u32[]{:S(2)}) copy-start(bf16[256,4096]{1,0:T(8,128)(2,1)} %param.17) | copy-start | bytes 6291460
  2.5 24.4 %all-to-all-start = ((bf16[16,128,128]{2,1,0:T(8,128)(2,1)}), bf16[16,128,128]{2,1,0:T(8,128)(2,1)S(1)}, u32[]{:S(2)}, u32[]{:S(2)}) async-start(bf16[16,128,128]{2,1,0:T(8,128)(2,1)} %broadcast_in_dim.21), calls=%async_computation | async-start | bytes 1048576 | tf_op jit(solution)/shard_map/all_to_all | solution.py:16
  38.1 15.2 %copy-start.6 = (s32[4,8]{1,0:T(4,128)S(1)}, s32[4,8]{1,0:T(4,128)}, u32[]{:S(2)}) copy-start(s32[4,8]{1,0:T(4,128)} %param.19) | copy-start | bytes 388
  38.1 15.6 %copy-start.7 = (f32[4,8]{1,0:T(4,128)S(1)}, f32[4,8]{1,0:T(4,128)}, u32[]{:S(2)}) copy-start(f32[4,8]{1,0:T(4,128)} %param.20) | copy-start | bytes 388
  38.1 32.1 %copy-start.4 = (bf16[4,4096]{1,0:T(4,128)(2,1)S(1)}, bf16[4,4096]{1,0:T(4,128)(2,1)}, u32[]{:S(2)}) copy-start(bf16[4,4096]{1,0:T(4,128)(2,1)} %param.16) | copy-start | bytes 98308
  38.1 32.3 %copy-start.5 = (f32[4096]{0:T(1024)S(1)}, f32[4096]{0:T(1024)}, u32[]{:S(2)}) copy-start(f32[4096]{0:T(1024)} %param.18) | copy-start | bytes 49156
  41.2 28.5 %all-to-all-start.3 = ((bf16[16,4,4096]{2,1,0:T(4,128)(2,1)}), bf16[16,4,4096]{2,1,0:T(4,128)(2,1)S(1)}, u32[]{:S(2)}, u32[]{:S(2)}) async-start(bf16[16,4,4096]{2,1,0:T(4,128)(2,1)} %reshape.157), calls=%async_computation.3 | async-start | bytes 1048576 | tf_op jit(solution)/shard_map/all_to_all | solution.py:16
  70.3 25.2 %copy-start.3 = (bf16[4,4096]{1,0:T(4,128)(2,1)}, bf16[4,4096]{1,0:T(4,128)(2,1)S(1)}, u32[]{:S(2)}) copy-start(bf16[4,4096]{1,0:T(4,128)(2,1)S(1)} %get-tuple-element.3) | copy-start | bytes 98308
  98.1 7.1 %copy-start.1 = (bf16[1,4096,96]{1,2,0:T(8,128)(2,1)S(1)}, bf16[1,4096,96]{1,2,0:T(8,128)(2,1)}, u32[]{:S(2)}) copy-start(bf16[1,4096,96]{1,2,0:T(8,128)(2,1)} %param.22) | copy-start | bytes 2359300
  98.1 104.9 %all-to-all-start.5 = ((bf16[8,64,4224]{2,1,0:T(8,128)(2,1)}), bf16[8,64,4224]{2,1,0:T(8,128)(2,1)}, u32[]{:S(2)}, u32[]{:S(2)}) async-start(bf16[8,64,4224]{2,1,0:T(8,128)(2,1)} %stack.21), calls=%async_computation.5 | async-start | bytes 8650752 | tf_op jit(solution)/shard_map/all_to_all | solution.py:114
  106.5 37.7 %collective-permute-start = (bf16[2,96,4096]{2,1,0:T(8,128)(2,1)S(1)}, bf16[2,96,4096]{2,1,0:T(8,128)(2,1)S(1)}, u32[]{:S(2)}, u32[]{:S(2)}) collective-permute-start(bf16[2,96,4096]{2,1,0:T(8,128)(2,1)S(1)} %get-tuple-element.7), channel_id=1, source_target_pairs={{0,256},{256,0},{1,257},{257,1},{2,258},{258,2},{3,259},{259,3},{4... | collective-permute-start | bytes 4718600 | tf_op jit(solution)/shard_map/ppermute | solution.py:76
  208.3 7.1 %copy-start.2 = (bf16[1,1536,256]{2,1,0:T(8,128)(2,1)S(1)}, bf16[1,1536,256]{2,1,0:T(8,128)(2,1)}, u32[]{:S(2)}) copy-start(bf16[1,1536,256]{2,1,0:T(8,128)(2,1)} %param.23) | copy-start | bytes 2359300
  209.6 42.1 %all-to-all-start.6 = ((bf16[8,192,512]{2,1,0:T(8,128)(2,1)}), bf16[8,192,512]{2,1,0:T(8,128)(2,1)}, u32[]{:S(2)}, u32[]{:S(2)}) async-start(bf16[8,192,512]{2,1,0:T(8,128)(2,1)} %broadcast_in_dim.31), calls=%async_computation.6 | async-start | bytes 3145728 | tf_op jit(solution)/shard_map/all_to_all | solution.py:16
  215.4 20.2 %collective-permute-start.1 = (bf16[1536,256]{1,0:T(8,128)(2,1)S(1)}, bf16[1536,256]{1,0:T(8,128)(2,1)}, u32[]{:S(2)}, u32[]{:S(2)}) collective-permute-start(bf16[1536,256]{1,0:T(8,128)(2,1)S(1)} %bitcast.79), channel_id=1, source_target_pairs={{0,256},{256,0},{1,257},{257,1},{2,258},{258,2},{3,259},{259,3},{4... | collective-permute-start | bytes 2359304 | tf_op jit(solution)/shard_map/ppermute | solution.py:77
  237.2 14.5 %copy-start.8 = (s32[1024]{0:T(1024)S(1)}, s32[1024]{0:T(1024)}, u32[]{:S(2)}) copy-start(s32[1024]{0:T(1024)} %constant.94.clone) | copy-start | bytes 12292
